TPU v7x, 32 devices: a whole 2x2x4 slice. The times are simulated.
32 devices in a mesh: space: 8 (over y, x, core), chan: 4 (over z).
Axes of the slice: x: 2, y: 2, z: 4, core: 2. Of those that a mesh axis runs over, the one named last changes fastest.
Arguments:
- activation: bfloat16 [8, 96, 16, 128], P('space', 'chan'), may hold values from -6 to 6
- weights: bfloat16 [3, 3, 3, 96, 96], replicated, may hold values from -0.125 to 0.125
- cotangent: bfloat16 [8, 96, 16, 128], P('space', 'chan'), may hold values from -6 to 6
Outputs:
- output: bfloat16 [8, 96, 16, 128], P('space', 'chan')
- input_grad: bfloat16 [8, 96, 16, 128], P('space', 'chan')
- weight_grad: float32 [3, 3, 3, 96, 96], P(None, None, None, None, 'chan')
All inputs are finite; a program needn't handle non-finite values.
Results may differ from a plain program's by a relative error of at most 0.0095.
Values may be sent and summed in bfloat16 or wider, within the bound.
A program may use at most 64 MiB of HBM per device.

v0:
```python
import math

import jax
import jax.numpy as jnp
from jax import lax
from jax.sharding import PartitionSpec as P


def extended(x, sides, width):
    for axis, dim in sides:
        size, length = (lax.axis_size(axis), x.shape[dim])
        up = [(i, (i + 1) % size) for i in range(size - 1)]
        down = [(j, i) for i, j in up]
        last = lax.slice_in_dim(x, length - width, length, axis=dim)
        leading = lax.slice_in_dim(x, 0, width, axis=dim)
        before = lax.ppermute(last, axis, up)
        after = lax.ppermute(leading, axis, down)
        x = jnp.concatenate([before, x, after], axis=dim)
    return x


def convolve(volume, kernel, depth_pad, layout):
    return lax.conv_general_dilated(
        volume,
        kernel,
        (1, 1, 1),
        (depth_pad, (1, 1), (1, 1)),
        dimension_numbers=layout,
        preferred_element_type=jnp.float32,
    )


def body(activation, weights, cotangent):
    planes, block, height_cells, width_cells = activation.shape
    channels = weights.shape[3]
    own_block = lax.axis_index("chan") * block
    total_cells = planes * lax.axis_size("space") * height_cells * width_cells
    out_cols = lax.dynamic_slice_in_dim(weights, own_block, block, 4)
    in_rows = lax.dynamic_slice_in_dim(weights, own_block, block, 3)
    stacked = jnp.stack((activation, cotangent))
    forward_layout = ("NDCHW", "DHWIO", "NDCHW")
    kernel_layout = ("CDNHW", "IDOHW", "NDHWC")
    grads_zero = jnp.zeros((3, 3, 3, channels, block), jnp.float32)
    padded = extended(stacked, (("space", 1),), 1)
    field_zero = jnp.zeros((planes, block, height_cells, width_cells), jnp.float32)
    shard_piece = lax.all_gather(padded, "chan", axis=2, tiled=True)
    source = shard_piece[0]
    signal = shard_piece[1]
    backward_w = jnp.flip(in_rows, (0, 1, 2))
    image = convolve(source[None], out_cols, (0, 0), forward_layout)[0]
    back = convolve(signal[None], backward_w, (0, 0), ("NDCHW", "DHWOI", "NDCHW"))[0]
    kernel_part = convolve(source[None], cotangent[None], (0, 0), kernel_layout)
    kernel_part = jnp.transpose(kernel_part, (1, 2, 3, 0, 4))
    grads = lax.dynamic_update_slice_in_dim(grads_zero, kernel_part, jnp.int32(0), 3)
    forward_sum = field_zero + image
    backward_sum = field_zero + back
    output = forward_sum.astype(jnp.bfloat16)
    input_grad = backward_sum.astype(jnp.bfloat16)
    weight_grad = lax.psum(grads, "space") / math.sqrt(total_cells)
    return (output, input_grad, weight_grad)


def solution(mesh):
    in_specs = (P("space", "chan", None, None), P(), P("space", "chan", None, None))
    out_specs = (
        P("space", "chan", None, None),
        P("space", "chan", None, None),
        P(None, None, None, None, "chan"),
    )
    return jax.shard_map(body, mesh=mesh, in_specs=in_specs, out_specs=out_specs, check_vma=False)
```

profile of v0, /device:TPU:13, one launch (start us, length us, event | category | flops | bytes accessed | tf_op | source)
XLA Modules:
  0.0 177.6 jit_solution(17397960274562948546)
XLA Ops:
  7.2 0.0 copy-start
  7.2 0.0 copy-start.2
  7.2 0.0 all-gather.2.cloned.1.call-start
  7.2 1.0 pad_maximum_fusion.1
  8.3 3.7 %collective-permute-start = (bf16[2,1,24,16,128]{4,3,2,1,0:T(8,128)(2,1)S(1)}, bf16[2,1,24,16,128]{4,3,2,1,0:T(8,128)(2,1)S(1)}, u32[]{:S(2)}, u32[]{:S(2)}) collective-permute-start(bf16[2,1,24,16,128]{4,3,2,1,0:T(8,128)(2,1)S(1)} %pad_maximum_fusion.1), channel_id=1, source_target_pairs={{0,4},{4,8},{8,12},{12,16},{16,20},{20,24},{24,28},{1,5},{5,9},{9,... | collective-permute-start | bytes 589832 | tf_op jit(solution)/shard_map/ppermute | solution.py:16
  11.9 1.9 %collective-permute-start.1 = (bf16[2,1,24,16,128]{4,3,2,1,0:T(8,128)(2,1)S(1)}, bf16[2,1,24,16,128]{4,3,2,1,0:T(8,128)(2,1)S(1)}, u32[]{:S(2)}, u32[]{:S(2)}) collective-permute-start(bf16[2,1,24,16,128]{4,3,2,1,0:T(8,128)(2,1)S(1)} %pad_maximum_fusion.1), channel_id=1, source_target_pairs={{4,0},{8,4},{12,8},{16,12},{20,16},{24,20},{28,24},{5,1},{9,5},{13... | collective-permute-start | bytes 589832 | tf_op jit(solution)/shard_map/ppermute | solution.py:17
  13.9 0.7 collective-permute-done
  14.5 4.4 %collective-permute-done.1 = bf16[2,1,24,16,128]{4,3,2,1,0:T(8,128)(2,1)S(1)} collective-permute-done((bf16[2,1,24,16,128]{4,3,2,1,0:T(8,128)(2,1)S(1)}, bf16[2,1,24,16,128]{4,3,2,1,0:T(8,128)(2,1)S(1)}, u32[]{:S(2)}, u32[]{:S(2)}) %collective-permute-start.1) | collective-permute-done | bytes 196640 | tf_op jit(solution)/shard_map/ppermute | solution.py:17
  18.9 1.0 pad_maximum_fusion
  19.9 0.9 copy.25
  20.9 0.0 all-gather.2.cloned.1.call-update
  20.9 0.0 all-reduce.2.cloned.1.call-start
  21.0 0.0 copy-done.2
  21.0 1.4 copy.38
  22.4 47.9 %all-gather.2.cloned.1.call-done = bf16[2,3,96,16,128]{4,3,1,0,2:T(8,128)(2,1)} async-done(((bf16[2,3,24,16,128]{4,3,1,0,2:T(8,128)(2,1)}), bf16[2,3,96,16,128]{4,3,1,0,2:T(8,128)(2,1)}) %all-gather.2.cloned.1.call-update) | async-done | bytes 2359312 | tf_op jit(solution)/shard_map/all_gather | solution.py:46
  70.3 3.1 %fusion.40 = (bf16[1,3,96,16,128]{4,3,1,0,2:T(8,128)(2,1)}, bf16[1,3,96,16,128]{4,3,1,0,2:T(8,128)(2,1)S(1)}) fusion(bf16[2,3,96,16,128]{4,3,1,0,2:T(8,128)(2,1)} %all-gather.2.cloned.1.call-done), kind=kLoop, calls=%fused_computation.38 | loop fusion | bytes 4718592 | tf_op jit(solution)/shard_map/slice | solution.py:48
  73.4 3.7 %copy.41 = bf16[1,3,96,16,128]{2,0,4,3,1:T(2,128)(2,1)} copy(bf16[1,3,96,16,128]{4,3,1,0,2:T(8,128)(2,1)S(1)} %get-tuple-element.10) | data formatting | bytes 2359296
  77.1 2.8 %copy_bitcast_fusion = (bf16[3,96,16,1,128]{4,2,1,0,3:T(8,128)(2,1)S(1)}, bf16[3,96,16,1,128]{4,2,1,0,3:T(8,128)(2,1)}) fusion(bf16[1,3,96,16,128]{4,3,1,0,2:T(8,128)(2,1)S(1)} %get-tuple-element.10, bf16[1,3,96,16,128]{4,3,1,0,2:T(8,128)(2,1)} %get-tuple-element.9), kind=kLoop, calls=%fused_computation.19 | loop fusion | bytes 4718592 | tf_op jit(solution)/shard_map/slice | solution.py:47
  79.9 2.4 %copy.45 = bf16[3,96,16,1,128]{1,2,4,0,3:T(8,128)(2,1)S(1)} copy(bf16[3,96,16,1,128]{4,2,1,0,3:T(8,128)(2,1)} %get-tuple-element.12) | data formatting | bytes 2359296
  82.3 0.3 pad.2.clone
  82.7 0.0 copy-start.3
  82.7 0.4 copy.36
  83.1 0.1 slice.16
  83.2 0.0 copy-done
  83.2 0.2 copy-done.3
  83.3 4.0 %fusion.19 = bf16[1,16,8,17,24]{4,2,3,1,0:T(8,128)(2,1)S(1)} fusion(bf16[3,96,16,1,7,2]{1,4,5,2,0,3:T(8,128)(2,1)S(1)} %slice.16, bf16[3,96,16,1,8,17]{1,4,5,2,0,3:T(8,128)(2,1)S(1)} %copy.36, pred[8,17]{0,1:T(8,128)(4,1)S(1)} %copy-done.3, bf16[3,3,3,96,96]{4,3,2,1,0:T(8,128)(2,1)S(1)} %copy-done, s32[]{:T(128)S(6)} %select_n.4), kind=kOutput, calls=%fused_computation.16 | convolution fusion | flops 263755776 | bytes 2141188 | tf_op jit(solution)/shard_map/conv_general_dilated | solution.py:23
  87.4 0.9 copy.37
  88.3 0.5 reshape.45
  88.8 0.7 copy.40
  89.5 1.7 copy.44
  91.2 0.3 pad.clone
  91.5 0.4 copy.30
  91.9 0.1 slice.13
  92.0 3.5 %fusion.25 = bf16[1,16,8,17,24]{4,2,3,1,0:T(8,128)(2,1)S(1)} fusion(bf16[3,96,16,1,7,2]{1,4,5,2,0,3:T(8,128)(2,1)S(1)} %slice.13, bf16[3,96,16,1,8,17]{1,4,5,2,0,3:T(8,128)(2,1)S(1)} %copy.30, bf16[3,3,3,96,96]{4,3,2,1,0:T(8,128)(2,1)S(1)} %copy-done, s32[]{:T(128)S(6)} %select_n.4, pred[8,17]{0,1:T(8,128)(4,1)S(1)} %copy-done.3), kind=kOutput, calls=%fused_computation.18 | convolution fusion | flops 263755776 | bytes 1984652 | tf_op jit(solution)/shard_map/conv_general_dilated | solution.py:23
  95.5 0.0 copy-start.1
  95.6 0.9 copy.32
  96.4 0.5 reshape.38
  97.0 0.0 copy-done.1
  97.0 19.0 %fusion.41 = f32[3,3,3,96,24]{3,4,2,1,0:T(8,128)} fusion(bf16[1,3,96,16,128]{2,0,4,3,1:T(2,128)(2,1)} %copy.41, bf16[1,1,24,16,128]{2,0,4,3,1:T(2,128)(2,1)S(1)} %copy-done.1), kind=kOutput, calls=%fused_computation.39 | convolution fusion | flops 242915328 | bytes 1526784 | tf_op jit(solution)/shard_map/transpose | solution.py:53
  116.0 0.0 all-reduce.2.cloned.1.call-update
  116.0 0.7 copy.39
  116.7 52.4 %all-reduce.2.cloned.1.call-done = f32[3,3,3,96,24]{3,4,2,1,0:T(8,128)} async-done(((f32[3,3,3,96,24]{3,4,2,1,0:T(8,128)}), f32[3,3,3,96,24]{3,4,2,1,0:T(8,128)}) %all-reduce.2.cloned.1.call-update) | async-done | bytes 248848 | tf_op jit(solution)/shard_map/psum | solution.py:59
  169.0 1.7 broadcast_multiply_fusion
  (2 shorter events, 0.0 us)
Async XLA Ops:
  7.2 76.0 %copy-start = (bf16[3,3,3,96,96]{4,3,2,1,0:T(8,128)(2,1)S(1)}, bf16[3,3,3,96,96]{4,3,2,1,0:T(8,128)(2,1)}, u32[]{:S(2)}) copy-start(bf16[3,3,3,96,96]{4,3,2,1,0:T(8,128)(2,1)} %param.4) | copy-start | bytes 1492996
  7.2 13.8 %copy-start.2 = (bf16[1,24,16,128]{3,2,1,0:T(8,128)(2,1)S(1)}, bf16[1,24,16,128]{3,2,1,0:T(8,128)(2,1)}, u32[]{:S(2)}) copy-start(bf16[1,24,16,128]{3,2,1,0:T(8,128)(2,1)} %param.5) | copy-start | bytes 294916
  7.2 63.1 %all-gather.2.cloned.1.call-start = ((), (), s32[]{:S(2)}) async-start(), calls=%async_computation | async-start | bytes 2949120 | tf_op jit(solution)/shard_map/all_gather | solution.py:46
  8.3 6.3 %collective-permute-start = (bf16[2,1,24,16,128]{4,3,2,1,0:T(8,128)(2,1)S(1)}, bf16[2,1,24,16,128]{4,3,2,1,0:T(8,128)(2,1)S(1)}, u32[]{:S(2)}, u32[]{:S(2)}) collective-permute-start(bf16[2,1,24,16,128]{4,3,2,1,0:T(8,128)(2,1)S(1)} %pad_maximum_fusion.1), channel_id=1, source_target_pairs={{0,4},{4,8},{8,12},{12,16},{16,20},{20,24},{24,28},{1,5},{5,9},{9,... | collective-permute-start | bytes 589832 | tf_op jit(solution)/shard_map/ppermute | solution.py:16
  11.9 7.0 %collective-permute-start.1 = (bf16[2,1,24,16,128]{4,3,2,1,0:T(8,128)(2,1)S(1)}, bf16[2,1,24,16,128]{4,3,2,1,0:T(8,128)(2,1)S(1)}, u32[]{:S(2)}, u32[]{:S(2)}) collective-permute-start(bf16[2,1,24,16,128]{4,3,2,1,0:T(8,128)(2,1)S(1)} %pad_maximum_fusion.1), channel_id=1, source_target_pairs={{4,0},{8,4},{12,8},{16,12},{20,16},{24,20},{28,24},{5,1},{9,5},{13... | collective-permute-start | bytes 589832 | tf_op jit(solution)/shard_map/ppermute | solution.py:17
  20.9 148.1 %all-reduce.2.cloned.1.call-start = ((), (), s32[]{:S(2)}) async-start(), calls=%async_computation.1 | async-start | bytes 663552 | tf_op jit(solution)/shard_map/psum | solution.py:59
  82.7 0.7 copy-start.3
  95.5 1.4 copy-start.1
Sparse Core Ops, SparseCore 0:
  21.0 49.1 all-gather.1
  116.1 52.8 all-reduce.1
where the time goes:
time: 180 us; the launch traced here: 178 us
  waiting for transfers between devices  105 us (58%)
  matrix products  26.6 us (15%)
  local copies, waits for them, and re-layouts  22 us (12%)
  between operations  14.2 us (8%)
  starting transfers between devices  5.68 us (3%)
  other arithmetic  3.75 us (2%)
    psum x1, waiting for transfers between devices, body(): weight_grad = lax.psum(grads, 'space') / math.sqrt(total_cells)  52.4 us
    all_gather x1, waiting for transfers between devices, body(): shard_piece = lax.all_gather(padded, 'chan', axis=2, tiled=True)  47.9 us
    transpose x1, matrix products, body(): kernel_part = jnp.transpose(kernel_part, (1, 2, 3, 0, 4))  19 us
    unnamed x13, local copies, waits for them, and re-layouts  9.33 us
    conv_general_dilated x2, matrix products, convolve(): lax.conv_general_dilated(volume, kernel, (1, 1, 1), (depth_pad, (1, 1), (...  7.58 us
    ppermute x1, waiting for transfers between devices, extended(): after = lax.ppermute(leading, axis, down)  4.4 us
    ppermute x1, starting transfers between devices, extended(): before = lax.ppermute(last, axis, up)  3.68 us
  transfers between devices with their start and end apart: 4, of which 4 were waited for; matrix products, arithmetic and copies ran while one was open for 1% of the time, Pallas kernels for 0%

commit v1 on v0

v1 whole, which is shorter than its diff:
```python
import functools
import math

import jax
import jax.numpy as jnp
from jax import lax
from jax.experimental import pallas as pl
from jax.experimental.pallas import tpu as pltpu
from jax.sharding import PartitionSpec as P

BF, F32 = jnp.bfloat16, jnp.float32
LANE = 128


def kernel(space, chan, blk, pad, channels, height, scale,
           a_ref, g_ref, w_ref, out_ref, back_ref, wg_ref,
           ga, gg, x3, gs, wf, wb, s32, t32, r32, z32,
           halo, psend, precv, own, wsend, wrecv, wcur,
           ga_s, ga_r, gg_s, gg_r, h_s, h_r, p_s, p_r, w_s, w_r):
    e = lax.axis_index("space")
    z = lax.axis_index("chan")
    rows = blk * height
    span = height * LANE
    rounds = space.bit_length() - 1
    up, down = lax.rem(e + 1, space), lax.rem(e + space - 1, space)

    def flip(bit):
        return e + bit * (1 - 2 * lax.rem(e // bit, 2))

    barrier = pltpu.get_barrier_semaphore()
    others = [{"chan": lax.rem(z + k, chan)} for k in range(1, chan)]
    others += [{"space": up}, {"space": down}]
    others += [{"space": flip(1 << r)} for r in range(rounds)]
    for other in others:
        pl.semaphore_signal(barrier, inc=1, device_id=other)
    pl.semaphore_wait(barrier, len(others))

    def gather(src, dst, ssem, rsem):
        return [
            pltpu.make_async_remote_copy(
                src, dst.at[z], ssem.at[k], rsem.at[k],
                device_id={"chan": lax.rem(z + k, chan)})
            for k in range(1, chan)
        ]

    def edge(src, dst, ssem, rsem, to):
        return pltpu.make_async_remote_copy(src, dst, ssem, rsem, device_id={"space": to})

    copies_a = gather(a_ref, ga, ga_s, ga_r)
    copies_g = gather(g_ref, gg, gg_s, gg_r)
    halo_up = edge(g_ref, halo.at[0], h_s.at[0], h_r.at[0], up)
    halo_down = edge(g_ref, halo.at[1], h_s.at[1], h_r.at[1], down)
    has_up, has_down = e < space - 1, e > 0

    for c in copies_a:
        c.start()
    pl.when(has_up)(halo_up.start)
    pl.when(has_down)(halo_down.start)
    for c in copies_g:
        c.start()

    def no_lower():
        halo[0] = jnp.zeros((rows, LANE), BF)
        precv[0] = jnp.zeros((rows, LANE), BF)
        precv[2] = jnp.zeros((rows, LANE), BF)

    def no_upper():
        halo[1] = jnp.zeros((rows, LANE), BF)
        precv[1] = jnp.zeros((rows, LANE), BF)
        precv[3] = jnp.zeros((rows, LANE), BF)

    pl.when(e == 0)(no_lower)
    pl.when(e == space - 1)(no_upper)
    ga[z] = a_ref[...]
    gg[z] = g_ref[...]

    x3[...] = jnp.zeros_like(x3)
    wf[...] = jnp.zeros_like(wf)
    wb[...] = jnp.zeros_like(wb)
    z32[...] = jnp.zeros_like(z32)
    row = lax.broadcasted_iota(jnp.int32, (pad, channels), 0)
    col = lax.broadcasted_iota(jnp.int32, (pad, channels), 1)
    pick = jnp.where((col == row + z * blk) & (row < blk), 1.0, 0.0).astype(BF)
    for a in range(3):
        for b in range(3):
            for c in range(3):
                at = (pl.ds((b * 3 + a) * pad, pad), pl.ds(c * LANE, channels))
                tap = w_ref[(a * 3 + b) * 3 + c]
                wf[at] = lax.dot_general(
                    pick, tap, (((1,), (1,)), ((), ())),
                    preferred_element_type=F32).astype(BF)
                tap = w_ref[26 - ((a * 3 + b) * 3 + c)]
                wb[at] = jnp.dot(pick, tap, preferred_element_type=F32).astype(BF)

    lane = lax.broadcasted_iota(jnp.int32, (channels * height, LANE), 1)

    def spread(src):
        v = src[...].reshape(channels * height, LANE).astype(F32)
        s32[0] = jnp.where(lane == 0, 0.0, pltpu.roll(v, 1, 1))
        s32[1] = v
        s32[2] = jnp.where(lane == LANE - 1, 0.0, pltpu.roll(v, LANE - 1, 1))
        for c in range(3):
            for h in range(height):
                x3[c * LANE:c * LANE + channels, (h + 1) * LANE:(h + 2) * LANE] = (
                    s32[c, pl.ds(h, channels, stride=height), :].astype(BF))

    def conv(w, slot, keep):
        r32[...] = jnp.dot(w[...], x3[:, LANE:LANE + span], preferred_element_type=F32)
        for a in range(3):
            for h in range(height):
                def part(b, hh):
                    return r32[(b * 3 + a) * pad:(b * 3 + a + 1) * pad, hh * LANE:(hh + 1) * LANE]
                v = part(1, h)
                if h > 0:
                    v = v + part(0, h - 1)
                if h < height - 1:
                    v = v + part(2, h + 1)
                t32[a, pl.ds(h, pad, stride=height), :] = v
        psend[slot] = t32[0, 0:rows, :].astype(BF)
        psend[slot + 1] = t32[2, 0:rows, :].astype(BF)
        own[keep] = t32[1, 0:rows, :]

    def partials(slot):
        return (edge(psend.at[slot], precv.at[slot], p_s.at[slot], p_r.at[slot], up),
                edge(psend.at[slot + 1], precv.at[slot + 1], p_s.at[slot + 1],
                     p_r.at[slot + 1], down))

    def finish(pair, slot, keep, ref):
        pl.when(has_down)(pair[0].wait_recv)
        pl.when(has_up)(pair[1].wait_recv)
        ref[...] = (own[keep] + precv[slot].astype(F32)
                    + precv[slot + 1].astype(F32)).astype(BF)

    for c in copies_a:
        c.wait_recv()
    spread(ga)
    conv(wf, 0, 0)
    pair_out = partials(0)
    pl.when(has_up)(pair_out[0].start)
    pl.when(has_down)(pair_out[1].start)

    pl.when(has_down)(halo_up.wait_recv)
    pl.when(has_up)(halo_down.wait_recv)
    for a in range(3):
        src = halo[1] if a == 0 else g_ref[...] if a == 1 else halo[0]
        z32[0:rows, :] = src.astype(F32)
        for h in range(height):
            gs[a * pad:(a + 1) * pad, h * LANE:(h + 1) * LANE] = (
                z32[pl.ds(h, pad, stride=height), :].astype(BF))
    for b in range(3):
        wcur[b] = lax.dot_general(
            gs[...], x3[:, b * LANE:b * LANE + span], (((1,), (1,)), ((), ())),
            preferred_element_type=F32)

    def exchange(r):
        return edge(wsend.at[r], wrecv.at[r], w_s.at[r], w_r.at[r], flip(1 << r))

    swaps = [exchange(r) for r in range(rounds)]

    def begin(r):
        wsend[r] = wcur[...].astype(BF)
        swaps[r].start()

    def end(r):
        swaps[r].wait_recv()
        wcur[...] = wsend[r].astype(F32) + wrecv[r].astype(F32)

    begin(0)
    end(0)
    if rounds > 1:
        begin(1)
    for c in copies_g:
        c.wait_recv()
    spread(gg)
    conv(wb, 2, 1)
    pair_back = partials(2)
    pl.when(has_up)(pair_back[0].start)
    pl.when(has_down)(pair_back[1].start)
    for r in range(1, rounds):
        end(r)
        if r + 1 < rounds:
            begin(r + 1)
        if r == 1:
            finish(pair_out, 0, 0, out_ref)
    if rounds < 2:
        finish(pair_out, 0, 0, out_ref)
    wg_ref[...] = wcur[...] * scale
    finish(pair_back, 2, 1, back_ref)

    for c in copies_a + copies_g + swaps:
        c.wait_send()
    for c in (halo_up, pair_out[0], pair_back[0]):
        pl.when(has_up)(c.wait_send)
    for c in (halo_down, pair_out[1], pair_back[1]):
        pl.when(has_down)(c.wait_send)


def body(space, chan, activation, weights, cotangent):
    planes, blk, height, width = activation.shape
    channels = weights.shape[3]
    assert planes == 1 and width == LANE and space & (space - 1) == 0
    pad = -(-blk // 16) * 16
    rows = blk * height
    rounds = space.bit_length() - 1
    scale = 1.0 / math.sqrt(planes * space * height * width)
    dma = pltpu.SemaphoreType.DMA
    vm = pltpu.VMEM
    wide = (height + 2) * LANE
    out, back, grads = pl.pallas_call(
        functools.partial(kernel, space, chan, blk, pad, channels, height, scale),
        out_shape=(
            jax.ShapeDtypeStruct((rows, LANE), BF),
            jax.ShapeDtypeStruct((rows, LANE), BF),
            jax.ShapeDtypeStruct((3, 3 * pad, 3 * LANE), F32),
        ),
        in_specs=[pl.BlockSpec(memory_space=pltpu.VMEM)] * 3,
        out_specs=[pl.BlockSpec(memory_space=pltpu.VMEM)] * 3,
        scratch_shapes=[
            vm((chan, rows, LANE), BF),
            vm((chan, rows, LANE), BF),
            vm((3 * LANE, wide), BF),
            vm((3 * pad, height * LANE), BF),
            vm((9 * pad, 3 * LANE), BF),
            vm((9 * pad, 3 * LANE), BF),
            vm((3, channels * height, LANE), F32),
            vm((3, pad * height, LANE), F32),
            vm((9 * pad, height * LANE), F32),
            vm((pad * height, LANE), F32),
            vm((2, rows, LANE), BF),
            vm((4, rows, LANE), BF),
            vm((4, rows, LANE), BF),
            vm((2, rows, LANE), F32),
            vm((rounds, 3, 3 * pad, 3 * LANE), BF),
            vm((rounds, 3, 3 * pad, 3 * LANE), BF),
            vm((3, 3 * pad, 3 * LANE), F32),
            dma((chan,)), dma((chan,)), dma((chan,)), dma((chan,)),
            dma((2,)), dma((2,)), dma((4,)), dma((4,)),
            dma((rounds,)), dma((rounds,)),
        ],
        compiler_params=pltpu.CompilerParams(
            collective_id=0, has_side_effects=True, vmem_limit_bytes=40 * 2**20),
    )(activation.reshape(rows, width), cotangent.reshape(rows, width),
      weights.reshape(27, channels, channels))
    field = (1, blk, height, width)
    grads = grads.reshape(3, 3, pad, 3, LANE)[:, :, :blk, :, :channels]
    grads = jnp.transpose(grads, (1, 0, 3, 4, 2))
    return out.reshape(field), back.reshape(field), grads


def solution(mesh):
    field = P("space", "chan", None, None)
    return jax.shard_map(
        functools.partial(body, mesh.shape["space"], mesh.shape["chan"]),
        mesh=mesh,
        in_specs=(field, P(), field),
        out_specs=(field, field, P(None, None, None, None, "chan")),
        check_vma=False,
    )
```

time: 180 us -> 42.1 us (0.23); the launches traced: 178 us -> 41.9 us
  waiting for transfers between devices: 105 us -> 0 us
  Pallas kernels: 0 us -> 36 us
  matrix products: 26.6 us -> 0 us
  local copies, waits for them, and re-layouts: 22 us -> 5.15 us
  between operations: 14.2 us -> 0.67 us
  starting transfers between devices: 5.68 us -> 0 us
  other arithmetic: 3.75 us -> 0 us
    psum x1 -> x0, waiting for transfers between devices: 52.4 us -> none  [body(): weight_grad = lax.psum(grads, 'space') / math.sqrt(total_cells)]
    all_gather x1 -> x0, waiting for transfers between devices: 47.9 us -> none  [body(): shard_piece = lax.all_gather(padded, 'chan', axis=2, tiled=True)]
    pallas_call x0 -> x1, Pallas kernels: none -> 36 us  [body(): pl.pallas_call(functools.partial(kernel, space, chan, blk, pad, channels,...]
    transpose x1 -> x0, matrix products: 19 us -> none  [body(): kernel_part = jnp.transpose(kernel_part, (1, 2, 3, 0, 4))]
    conv_general_dilated x2 -> x0, matrix products: 7.58 us -> none  [convolve(): lax.conv_general_dilated(volume, kernel, (1, 1, 1), (depth_pad, (1, 1), (...]
    slice x4 -> x0, local copies, waits for them, and re-layouts: 6.53 us -> none  [the longest x2 3.4 us: body(): signal = shard_piece[1]]
    ppermute x2 -> x0, starting transfers between devices: 5.6 us -> none  [the longest x1 3.68 us: extended(): before = lax.ppermute(last, axis, up)]
    ppermute x2 -> x0, waiting for transfers between devices: 5.06 us -> none  [the longest x1 4.4 us: extended(): after = lax.ppermute(leading, axis, down)]
  transfers between devices with their start and end apart: 4 -> 0, of which waited for: 4 -> 0; matrix products, arithmetic and copies ran while one was open for 1% -> 0% of each run, Pallas kernels for 0% -> 0%
where the time goes in v1:
time: 42.1 us; the launch traced here: 41.9 us
  Pallas kernels  36 us (86%)
  local copies, waits for them, and re-layouts  5.15 us (12%)
  between operations  0.67 us (2%)
    pallas_call x1, Pallas kernels, body(): pl.pallas_call(functools.partial(kernel, space, chan, blk, pad, channels,...  36 us
    unnamed x9, local copies, waits for them, and re-layouts  4.9 us

profile of v1, /device:TPU:13, one launch (start us, length us, event | category | flops | bytes accessed | tf_op | source)
XLA Modules:
  0.0 41.9 jit_solution(2953261663690996995)
XLA Ops:
  0.6 0.0 copy-start
  0.6 1.1 %copy-done = bf16[3,3,3,96,96]{4,3,2,1,0:T(8,128)(2,1)S(1)} copy-done((bf16[3,3,3,96,96]{4,3,2,1,0:T(8,128)(2,1)S(1)}, bf16[3,3,3,96,96]{4,3,2,1,0:T(8,128)(2,1)}, u32[]{:S(2)}) %copy-start) | copy-done | bytes 497688
  1.7 0.0 copy-start.1
  1.7 0.9 %copy-done.1 = bf16[1,24,16,128]{3,2,1,0:T(8,128)(2,1)S(1)} copy-done((bf16[1,24,16,128]{3,2,1,0:T(8,128)(2,1)S(1)}, bf16[1,24,16,128]{3,2,1,0:T(8,128)(2,1)}, u32[]{:S(2)}) %copy-start.1) | copy-done | bytes 98328
  2.6 0.0 copy-start.2
  2.6 0.9 %copy-done.2 = bf16[1,24,16,128]{3,2,1,0:T(8,128)(2,1)S(1)} copy-done((bf16[1,24,16,128]{3,2,1,0:T(8,128)(2,1)S(1)}, bf16[1,24,16,128]{3,2,1,0:T(8,128)(2,1)}, u32[]{:S(2)}) %copy-start.2) | copy-done | bytes 98328
  3.5 36.0 %shard_map.58 = (bf16[384,128]{1,0:T(8,128)(2,1)S(1)}, bf16[384,128]{1,0:T(8,128)(2,1)S(1)}, f32[3,96,384]{2,1,0:T(8,128)S(1)}) custom-call(bf16[384,128]{1,0:T(8,128)(2,1)S(1)} %bitcast.10, bf16[384,128]{1,0:T(8,128)(2,1)S(1)} %bitcast.11, bf16[27,96,96]{2,1,0:T(8,128)(2,1)S(1)} %bitcast.7), custom_call_target="tpu_custom_call" | custom-call | tf_op jit(solution)/shard_map/pallas_call | solution.py:209
  39.6 0.2 reshape.29
  39.7 0.1 slice_bitcast_fusion
  39.8 0.8 %copy.7 = f32[3,3,3,96,24]{3,4,2,1,0:T(8,128)} copy(f32[3,3,3,96,24]{3,2,4,0,1:T(4,128)S(1)} %slice_bitcast_fusion) | data formatting | bytes 497664
  40.6 0.6 %copy.10 = bf16[1,24,16,128]{3,2,1,0:T(8,128)(2,1)} copy(bf16[1,24,16,128]{3,2,1,0:T(8,128)(2,1)S(1)} %bitcast.9) | data formatting | bytes 196608
  41.2 0.6 %copy.11 = bf16[1,24,16,128]{3,2,1,0:T(8,128)(2,1)} copy(bf16[1,24,16,128]{3,2,1,0:T(8,128)(2,1)S(1)} %bitcast.8) | data formatting | bytes 196608
Async XLA Ops:
  0.6 1.1 %copy-start = (bf16[3,3,3,96,96]{4,3,2,1,0:T(8,128)(2,1)S(1)}, bf16[3,3,3,96,96]{4,3,2,1,0:T(8,128)(2,1)}, u32[]{:S(2)}) copy-start(bf16[3,3,3,96,96]{4,3,2,1,0:T(8,128)(2,1)} %param.4) | copy-start | bytes 1492996
  1.7 0.9 %copy-start.1 = (bf16[1,24,16,128]{3,2,1,0:T(8,128)(2,1)S(1)}, bf16[1,24,16,128]{3,2,1,0:T(8,128)(2,1)}, u32[]{:S(2)}) copy-start(bf16[1,24,16,128]{3,2,1,0:T(8,128)(2,1)} %param.3) | copy-start | bytes 294916
  2.6 0.9 %copy-start.2 = (bf16[1,24,16,128]{3,2,1,0:T(8,128)(2,1)S(1)}, bf16[1,24,16,128]{3,2,1,0:T(8,128)(2,1)}, u32[]{:S(2)}) copy-start(bf16[1,24,16,128]{3,2,1,0:T(8,128)(2,1)} %param.5) | copy-start | bytes 294916

commit v2 on v0

v2 whole, which is shorter than its diff:
```python
import functools
import math

import jax
import jax.numpy as jnp
from jax import lax
from jax.experimental import pallas as pl
from jax.experimental.pallas import tpu as pltpu
from jax.sharding import PartitionSpec as P

BF, F32 = jnp.bfloat16, jnp.float32
LANE = 128


def kernel(space, chan, blk, pad, channels, height, scale,
           a_ref, g_ref, w_ref, out_ref, back_ref, wg_ref,
           ga, x3, xg, wf, wb, s32, t32, r32, z32, part,
           halo, psend, precv, wflat, wsend, wrecv, wfull,
           rsend, rrecv,
           g_s, g_r, h_s, h_r, p_s, p_r, w_s, w_r, f_s, f_r, r_s, r_r):
    e = lax.axis_index("space")
    z = lax.axis_index("chan")
    rows = blk * height
    span = height * LANE
    up, down = lax.rem(e + 1, space), lax.rem(e + space - 1, space)

    def along_z(k):
        return lax.rem(z + k, chan)

    def along_e(k):
        return lax.rem(e + k, space)

    barrier = pltpu.get_barrier_semaphore()
    others = [{"chan": along_z(k)} for k in range(1, chan)]
    others += [{"space": along_e(k)} for k in range(1, space)]
    for other in others:
        pl.semaphore_signal(barrier, inc=1, device_id=other)
    pl.semaphore_wait(barrier, len(others))

    def send(src, dst, ssem, rsem, to):
        return pltpu.make_async_remote_copy(src, dst, ssem, rsem, device_id=to)

    gathers = [send(a_ref, ga.at[z], g_s.at[k], g_r.at[k], {"chan": along_z(k)})
               for k in range(1, chan)]

    halo_up = send(g_ref, halo.at[0], h_s.at[0], h_r.at[0], {"space": up})
    halo_down = send(g_ref, halo.at[1], h_s.at[1], h_r.at[1], {"space": down})
    has_up, has_down = e < space - 1, e > 0

    for c in gathers:
        c.start()
    pl.when(has_up)(halo_up.start)
    pl.when(has_down)(halo_down.start)

    def no_lower():
        halo[0] = jnp.zeros((rows, LANE), BF)
        precv[0] = jnp.zeros((rows, LANE), BF)

    def no_upper():
        halo[1] = jnp.zeros((rows, LANE), BF)
        precv[1] = jnp.zeros((rows, LANE), BF)

    pl.when(e == 0)(no_lower)
    pl.when(e == space - 1)(no_upper)
    ga[z] = a_ref[...]

    wide = 9 * pad
    first = lax.broadcasted_iota(jnp.int32, (channels, wide), 0) - z * blk
    place = lax.broadcasted_iota(jnp.int32, (channels, wide), 1)
    inside = (first >= 0) & (first < blk)
    for b in range(3):
        total = jnp.zeros((channels, wide), F32)
        for c in range(3):
            for a in range(3):
                spot = inside & (place == first + (c * 3 + a) * pad)
                tap = w_ref[(a * 3 + 2 - b) * 3 + 2 - c]
                total = total + jnp.dot(
                    tap, jnp.where(spot, 1.0, 0.0).astype(BF), preferred_element_type=F32)
        wb[b * channels:(b + 1) * channels, :] = total.astype(BF)

    z32[...] = jnp.zeros_like(z32)
    few = lax.broadcasted_iota(jnp.int32, (rows, LANE), 1)

    def fill(a, src):
        v = src.astype(F32)
        z32[0, 0:rows, :] = jnp.where(few == 0, 0.0, pltpu.roll(v, 1, 1))
        z32[1, 0:rows, :] = v
        z32[2, 0:rows, :] = jnp.where(few == LANE - 1, 0.0, pltpu.roll(v, LANE - 1, 1))
        for c in range(3):
            at = (c * 3 + a) * pad
            for h in range(height):
                xg[at:at + pad, h * LANE:(h + 1) * LANE] = (
                    z32[c, pl.ds(h, pad, stride=height), :].astype(BF))

    fill(1, g_ref[...])
    pl.when(has_down)(halo_up.wait_recv)
    fill(2, halo[0])
    pl.when(has_up)(halo_down.wait_recv)
    fill(0, halo[1])

    def shifted(count, first_row, group, h):
        def piece(b, hh):
            at = first_row + b * group
            return r32[at:at + count, hh * LANE:(hh + 1) * LANE]
        v = piece(1, h)
        if h > 0:
            v = v + piece(0, h - 1)
        if h < height - 1:
            v = v + piece(2, h + 1)
        return v

    r32[0:3 * channels, :] = jnp.dot(wb[...], xg[...], preferred_element_type=F32)
    for h in range(height):
        part[pl.ds(h, channels, stride=height), :] = shifted(channels, 0, channels, h)

    sums = [send(rsend.at[k], rrecv.at[k], r_s.at[k], r_r.at[k], {"chan": along_z(k)})
            for k in range(1, chan)]

    def block(t):
        return part[pl.ds(pl.multiple_of(t * rows, 16), rows), :]

    for k in range(1, chan):
        rsend[k] = block(along_z(k)).astype(BF)
        sums[k - 1].start()

    x3[...] = jnp.zeros_like(x3)
    wf[...] = jnp.zeros_like(wf)
    row = lax.broadcasted_iota(jnp.int32, (pad, channels), 0)
    col = lax.broadcasted_iota(jnp.int32, (pad, channels), 1)
    pick = jnp.where((col == row + z * blk) & (row < blk), 1.0, 0.0).astype(BF)
    for a in range(3):
        for b in range(3):
            for c in range(3):
                wf[pl.ds((b * 3 + a) * pad, pad), pl.ds(c * LANE, channels)] = (
                    lax.dot_general(
                        pick, w_ref[(a * 3 + b) * 3 + c], (((1,), (1,)), ((), ())),
                        preferred_element_type=F32).astype(BF))

    for c in gathers:
        c.wait_recv()
    lane = lax.broadcasted_iota(jnp.int32, (channels * height, LANE), 1)
    v = ga[...].reshape(channels * height, LANE).astype(F32)
    s32[0] = jnp.where(lane == 0, 0.0, pltpu.roll(v, 1, 1))
    s32[1] = v
    s32[2] = jnp.where(lane == LANE - 1, 0.0, pltpu.roll(v, LANE - 1, 1))
    for c in range(3):
        for h in range(height):
            x3[c * LANE:c * LANE + channels, (h + 1) * LANE:(h + 2) * LANE] = (
                s32[c, pl.ds(h, channels, stride=height), :].astype(BF))

    signal = xg[3 * pad:6 * pad, :]
    for b in range(3):
        share = lax.dot_general(
            signal, x3[:, b * LANE:b * LANE + span], (((1,), (1,)), ((), ())),
            preferred_element_type=F32)
        for c in range(3):
            at = (c * 9 + b * 3) * pad
            wflat[at:at + 3 * pad, :] = share[:, c * LANE:(c + 1) * LANE]
    total_rows = wflat.shape[0]
    chunk = total_rows // space
    if total_rows > 27 * pad:
        wflat[27 * pad:total_rows, :] = jnp.zeros((total_rows - 27 * pad, LANE), F32)
    wsend[...] = wflat[...].astype(BF).reshape(space, chunk, LANE)
    shares = [send(wsend.at[along_e(k)], wrecv.at[k], w_s.at[k], w_r.at[k],
                   {"space": along_e(k)}) for k in range(1, space)]
    for c in shares:
        c.start()

    r32[0:9 * pad, :] = jnp.dot(wf[...], x3[:, LANE:LANE + span], preferred_element_type=F32)

    def relay(a):
        for h in range(height):
            t32[a, pl.ds(h, pad, stride=height), :] = shifted(pad, a * pad, 3 * pad, h)

    relay(0)
    psend[0] = t32[0, 0:rows, :].astype(BF)
    pair = (send(psend.at[0], precv.at[0], p_s.at[0], p_r.at[0], {"space": up}),
            send(psend.at[1], precv.at[1], p_s.at[1], p_r.at[1], {"space": down}))
    pl.when(has_up)(pair[0].start)
    relay(2)
    psend[1] = t32[2, 0:rows, :].astype(BF)
    pl.when(has_down)(pair[1].start)

    relay(1)
    for c in shares:
        c.wait_recv()
    mine = wflat[pl.ds(pl.multiple_of(e * chunk, 16), chunk), :]
    for k in range(1, space):
        mine = mine + wrecv[k].astype(F32)
    wfull[e] = mine.astype(BF)
    fulls = [send(wfull.at[e], wfull.at[e], f_s.at[k], f_r.at[k], {"space": along_e(k)})
             for k in range(1, space)]
    for c in fulls:
        c.start()

    pl.when(has_down)(pair[0].wait_recv)
    pl.when(has_up)(pair[1].wait_recv)
    out_ref[...] = (t32[1, 0:rows, :] + precv[0].astype(F32)
                    + precv[1].astype(F32)).astype(BF)

    for c in sums:
        c.wait_recv()
    total = block(z)
    for k in range(1, chan):
        total = total + rrecv[k].astype(F32)
    back_ref[...] = total.astype(BF)

    for c in fulls:
        c.wait_recv()
    wflat[...] = wfull[...].reshape(total_rows, LANE).astype(F32) * scale
    for a in range(3):
        for b in range(3):
            for c in range(3):
                at = (c * 9 + b * 3 + a) * pad
                wg_ref[(a * 3 + b) * 3 + c] = wflat[at:at + blk, 0:channels]

    for c in gathers + sums + shares + fulls:
        c.wait_send()
    for c in (halo_up, pair[0]):
        pl.when(has_up)(c.wait_send)
    for c in (halo_down, pair[1]):
        pl.when(has_down)(c.wait_send)


def body(space, chan, activation, weights, cotangent):
    planes, blk, height, width = activation.shape
    channels = weights.shape[3]
    assert planes == 1 and width == LANE
    pad = -(-blk // 16) * 16
    rows = blk * height
    scale = 1.0 / math.sqrt(planes * space * height * width)
    dma = pltpu.SemaphoreType.DMA
    vm = pltpu.VMEM
    wide = (height + 2) * LANE
    chunk = -(-27 * pad // (16 * space)) * 16
    out, back, grads = pl.pallas_call(
        functools.partial(kernel, space, chan, blk, pad, channels, height, scale),
        out_shape=(
            jax.ShapeDtypeStruct((rows, LANE), BF),
            jax.ShapeDtypeStruct((rows, LANE), BF),
            jax.ShapeDtypeStruct((27, blk, channels), F32),
        ),
        in_specs=[pl.BlockSpec(memory_space=pltpu.VMEM)] * 3,
        out_specs=[pl.BlockSpec(memory_space=pltpu.VMEM)] * 3,
        scratch_shapes=[
            vm((chan, rows, LANE), BF),
            vm((3 * LANE, wide), BF),
            vm((9 * pad, height * LANE), BF),
            vm((9 * pad, 3 * LANE), BF),
            vm((3 * channels, 9 * pad), BF),
            vm((3, channels * height, LANE), F32),
            vm((3, pad * height, LANE), F32),
            vm((max(9 * pad, 3 * channels), height * LANE), F32),
            vm((3, pad * height, LANE), F32),
            vm((channels * height, LANE), F32),
            vm((2, rows, LANE), BF),
            vm((2, rows, LANE), BF),
            vm((2, rows, LANE), BF),
            vm((space * chunk, LANE), F32),
            vm((space, chunk, LANE), BF),
            vm((space, chunk, LANE), BF),
            vm((space, chunk, LANE), BF),
            vm((chan, rows, LANE), BF),
            vm((chan, rows, LANE), BF),
            dma((chan,)), dma((chan,)), dma((2,)), dma((2,)), dma((2,)), dma((2,)),
            dma((space,)), dma((space,)), dma((space,)), dma((space,)),
            dma((chan,)), dma((chan,)),
        ],
        compiler_params=pltpu.CompilerParams(
            collective_id=0, has_side_effects=True, vmem_limit_bytes=40 * 2**20),
    )(activation.reshape(rows, width), cotangent.reshape(rows, width),
      weights.reshape(27, channels, channels))
    field = (1, blk, height, width)
    grads = jnp.swapaxes(grads.reshape(3, 3, 3, blk, channels), 3, 4)
    return out.reshape(field), back.reshape(field), grads


def solution(mesh):
    field = P("space", "chan", None, None)
    return jax.shard_map(
        functools.partial(body, mesh.shape["space"], mesh.shape["chan"]),
        mesh=mesh,
        in_specs=(field, P(), field),
        out_specs=(field, field, P(None, None, None, None, "chan")),
        check_vma=False,
    )
```

time: 180 us -> 35.6 us (0.20); the launches traced: 178 us -> 35.2 us
  waiting for transfers between devices: 105 us -> 0 us
  Pallas kernels: 0 us -> 29.7 us
  matrix products: 26.6 us -> 0 us
  local copies, waits for them, and re-layouts: 22 us -> 4.88 us
  between operations: 14.2 us -> 0.65 us
  starting transfers between devices: 5.68 us -> 0 us
  other arithmetic: 3.75 us -> 0 us
    psum x1 -> x0, waiting for transfers between devices: 52.4 us -> none  [body(): weight_grad = lax.psum(grads, 'space') / math.sqrt(total_cells)]
    all_gather x1 -> x0, waiting for transfers between devices: 47.9 us -> none  [body(): shard_piece = lax.all_gather(padded, 'chan', axis=2, tiled=True)]
    pallas_call x0 -> x1, Pallas kernels: none -> 29.7 us  [body(): pl.pallas_call(functools.partial(kernel, space, chan, blk, pad, channels,...]
    transpose x1 -> x0, matrix products: 19 us -> none  [body(): kernel_part = jnp.transpose(kernel_part, (1, 2, 3, 0, 4))]
    conv_general_dilated x2 -> x0, matrix products: 7.58 us -> none  [convolve(): lax.conv_general_dilated(volume, kernel, (1, 1, 1), (depth_pad, (1, 1), (...]
    slice x4 -> x0, local copies, waits for them, and re-layouts: 6.53 us -> none  [the longest x2 3.4 us: body(): signal = shard_piece[1]]
    ppermute x2 -> x0, starting transfers between devices: 5.6 us -> none  [the longest x1 3.68 us: extended(): before = lax.ppermute(last, axis, up)]
    ppermute x2 -> x0, waiting for transfers between devices: 5.06 us -> none  [the longest x1 4.4 us: extended(): after = lax.ppermute(leading, axis, down)]
  transfers between devices with their start and end apart: 4 -> 0, of which waited for: 4 -> 0; matrix products, arithmetic and copies ran while one was open for 1% -> 0% of each run, Pallas kernels for 0% -> 0%
where the time goes in v2:
time: 35.6 us; the launch traced here: 35.2 us
  Pallas kernels  29.7 us (83%)
  local copies, waits for them, and re-layouts  4.88 us (14%)
  between operations  0.65 us (2%)
    pallas_call x1, Pallas kernels, body(): pl.pallas_call(functools.partial(kernel, space, chan, blk, pad, channels,...  29.7 us
    unnamed x9, local copies, waits for them, and re-layouts  4.88 us

profile of v2, /device:TPU:13, one launch (start us, length us, event | category | flops | bytes accessed | tf_op | source)
XLA Modules:
  0.0 35.2 jit_solution(10119355627200453384)
XLA Ops:
  0.6 0.0 copy-start
  0.6 1.1 %copy-done = bf16[3,3,3,96,96]{4,3,2,1,0:T(8,128)(2,1)S(1)} copy-done((bf16[3,3,3,96,96]{4,3,2,1,0:T(8,128)(2,1)S(1)}, bf16[3,3,3,96,96]{4,3,2,1,0:T(8,128)(2,1)}, u32[]{:S(2)}) %copy-start) | copy-done | bytes 497688
  1.7 0.0 copy-start.1
  1.7 0.9 %copy-done.1 = bf16[1,24,16,128]{3,2,1,0:T(8,128)(2,1)S(1)} copy-done((bf16[1,24,16,128]{3,2,1,0:T(8,128)(2,1)S(1)}, bf16[1,24,16,128]{3,2,1,0:T(8,128)(2,1)}, u32[]{:S(2)}) %copy-start.1) | copy-done | bytes 98328
  2.6 0.0 copy-start.2
  2.6 0.9 %copy-done.2 = bf16[1,24,16,128]{3,2,1,0:T(8,128)(2,1)S(1)} copy-done((bf16[1,24,16,128]{3,2,1,0:T(8,128)(2,1)S(1)}, bf16[1,24,16,128]{3,2,1,0:T(8,128)(2,1)}, u32[]{:S(2)}) %copy-start.2) | copy-done | bytes 98328
  3.5 29.7 %shard_map.58 = (bf16[384,128]{1,0:T(8,128)(2,1)S(1)}, bf16[384,128]{1,0:T(8,128)(2,1)S(1)}, f32[27,24,96]{2,1,0:T(8,128)S(1)}) custom-call(bf16[384,128]{1,0:T(8,128)(2,1)S(1)} %bitcast.12, bf16[384,128]{1,0:T(8,128)(2,1)S(1)} %bitcast.13, bf16[27,96,96]{2,1,0:T(8,128)(2,1)S(1)} %bitcast.8), custom_call_target="tpu_custom_call" | custom-call | tf_op jit(solution)/shard_map/pallas_call | solution.py:236
  33.2 0.6 %copy.9 = bf16[1,24,16,128]{3,2,1,0:T(8,128)(2,1)} copy(bf16[1,24,16,128]{3,2,1,0:T(8,128)(2,1)S(1)} %bitcast.11) | data formatting | bytes 196608
  33.8 0.6 %copy.10 = bf16[1,24,16,128]{3,2,1,0:T(8,128)(2,1)} copy(bf16[1,24,16,128]{3,2,1,0:T(8,128)(2,1)S(1)} %bitcast.10) | data formatting | bytes 196608
  34.5 0.7 %copy.11 = f32[3,3,3,96,24]{3,4,2,1,0:T(8,128)} copy(f32[3,3,3,96,24]{3,4,2,1,0:T(8,128)S(1)} %bitcast.9) | data formatting | bytes 497664
Async XLA Ops:
  0.6 1.1 %copy-start = (bf16[3,3,3,96,96]{4,3,2,1,0:T(8,128)(2,1)S(1)}, bf16[3,3,3,96,96]{4,3,2,1,0:T(8,128)(2,1)}, u32[]{:S(2)}) copy-start(bf16[3,3,3,96,96]{4,3,2,1,0:T(8,128)(2,1)} %param.4) | copy-start | bytes 1492996
  1.7 0.9 %copy-start.1 = (bf16[1,24,16,128]{3,2,1,0:T(8,128)(2,1)S(1)}, bf16[1,24,16,128]{3,2,1,0:T(8,128)(2,1)}, u32[]{:S(2)}) copy-start(bf16[1,24,16,128]{3,2,1,0:T(8,128)(2,1)} %param.3) | copy-start | bytes 294916
  2.6 0.9 %copy-start.2 = (bf16[1,24,16,128]{3,2,1,0:T(8,128)(2,1)S(1)}, bf16[1,24,16,128]{3,2,1,0:T(8,128)(2,1)}, u32[]{:S(2)}) copy-start(bf16[1,24,16,128]{3,2,1,0:T(8,128)(2,1)} %param.5) | copy-start | bytes 294916

commit v3 on v2

--- a/solution.py
+++ b/solution.py
@@ -121,7 +121,6 @@
 
     for k in range(1, chan):
         rsend[k] = block(along_z(k)).astype(BF)
-        sums[k - 1].start()
 
     x3[...] = jnp.zeros_like(x3)
     wf[...] = jnp.zeros_like(wf)
@@ -138,6 +137,8 @@
 
     for c in gathers:
         c.wait_recv()
+    for c in sums:
+        c.start()
     lane = lax.broadcasted_iota(jnp.int32, (channels * height, LANE), 1)
     v = ga[...].reshape(channels * height, LANE).astype(F32)
     s32[0] = jnp.where(lane == 0, 0.0, pltpu.roll(v, 1, 1))

time: 35.6 us -> 31.5 us (0.88)
  Pallas kernels: 29.7 us -> 25.5 us
    pallas_call x1, Pallas kernels: 29.7 us -> 25.5 us  [body(): pl.pallas_call(functools.partial(kernel, space, chan, blk, pad, channels,...]
where the time goes in v3:
time: 31.5 us; the launch traced here: 31 us
  Pallas kernels  25.5 us (81%)
  local copies, waits for them, and re-layouts  4.88 us (15%)
  between operations  0.65 us (2%)
    pallas_call x1, Pallas kernels, body(): pl.pallas_call(functools.partial(kernel, space, chan, blk, pad, channels,...  25.5 us
    unnamed x9, local copies, waits for them, and re-layouts  4.88 us

profile of v3, /device:TPU:13, one launch (start us, length us, event | category | flops | bytes accessed | tf_op | source)
XLA Modules:
  0.0 31.0 jit_solution(4233962289419288722)
XLA Ops:
  0.6 0.0 copy-start
  0.6 1.1 %copy-done = bf16[3,3,3,96,96]{4,3,2,1,0:T(8,128)(2,1)S(1)} copy-done((bf16[3,3,3,96,96]{4,3,2,1,0:T(8,128)(2,1)S(1)}, bf16[3,3,3,96,96]{4,3,2,1,0:T(8,128)(2,1)}, u32[]{:S(2)}) %copy-start) | copy-done | bytes 497688
  1.7 0.0 copy-start.1
  1.7 0.9 %copy-done.1 = bf16[1,24,16,128]{3,2,1,0:T(8,128)(2,1)S(1)} copy-done((bf16[1,24,16,128]{3,2,1,0:T(8,128)(2,1)S(1)}, bf16[1,24,16,128]{3,2,1,0:T(8,128)(2,1)}, u32[]{:S(2)}) %copy-start.1) | copy-done | bytes 98328
  2.6 0.0 copy-start.2
  2.6 0.9 %copy-done.2 = bf16[1,24,16,128]{3,2,1,0:T(8,128)(2,1)S(1)} copy-done((bf16[1,24,16,128]{3,2,1,0:T(8,128)(2,1)S(1)}, bf16[1,24,16,128]{3,2,1,0:T(8,128)(2,1)}, u32[]{:S(2)}) %copy-start.2) | copy-done | bytes 98328
  3.5 25.5 %shard_map.58 = (bf16[384,128]{1,0:T(8,128)(2,1)S(1)}, bf16[384,128]{1,0:T(8,128)(2,1)S(1)}, f32[27,24,96]{2,1,0:T(8,128)S(1)}) custom-call(bf16[384,128]{1,0:T(8,128)(2,1)S(1)} %bitcast.12, bf16[384,128]{1,0:T(8,128)(2,1)S(1)} %bitcast.13, bf16[27,96,96]{2,1,0:T(8,128)(2,1)S(1)} %bitcast.8), custom_call_target="tpu_custom_call" | custom-call | tf_op jit(solution)/shard_map/pallas_call | solution.py:237
  29.0 0.6 %copy.9 = bf16[1,24,16,128]{3,2,1,0:T(8,128)(2,1)} copy(bf16[1,24,16,128]{3,2,1,0:T(8,128)(2,1)S(1)} %bitcast.11) | data formatting | bytes 196608
  29.7 0.6 %copy.10 = bf16[1,24,16,128]{3,2,1,0:T(8,128)(2,1)} copy(bf16[1,24,16,128]{3,2,1,0:T(8,128)(2,1)S(1)} %bitcast.10) | data formatting | bytes 196608
  30.3 0.7 %copy.11 = f32[3,3,3,96,24]{3,4,2,1,0:T(8,128)} copy(f32[3,3,3,96,24]{3,4,2,1,0:T(8,128)S(1)} %bitcast.9) | data formatting | bytes 497664
Async XLA Ops:
  0.6 1.1 %copy-start = (bf16[3,3,3,96,96]{4,3,2,1,0:T(8,128)(2,1)S(1)}, bf16[3,3,3,96,96]{4,3,2,1,0:T(8,128)(2,1)}, u32[]{:S(2)}) copy-start(bf16[3,3,3,96,96]{4,3,2,1,0:T(8,128)(2,1)} %param.4) | copy-start | bytes 1492996
  1.7 0.9 %copy-start.1 = (bf16[1,24,16,128]{3,2,1,0:T(8,128)(2,1)S(1)}, bf16[1,24,16,128]{3,2,1,0:T(8,128)(2,1)}, u32[]{:S(2)}) copy-start(bf16[1,24,16,128]{3,2,1,0:T(8,128)(2,1)} %param.3) | copy-start | bytes 294916
  2.6 0.9 %copy-start.2 = (bf16[1,24,16,128]{3,2,1,0:T(8,128)(2,1)S(1)}, bf16[1,24,16,128]{3,2,1,0:T(8,128)(2,1)}, u32[]{:S(2)}) copy-start(bf16[1,24,16,128]{3,2,1,0:T(8,128)(2,1)} %param.5) | copy-start | bytes 294916
